TPU v7x, 32 devices: a whole 2x2x4 slice. The times are simulated.
32 devices in a mesh: cuts: 4 (over y, core), bita: 4 (over z), bitb: 2 (over x).
Axes of the slice: x: 2, y: 2, z: 4, core: 2. Of those that a mesh axis runs over, the one named last changes fastest.
Arguments:
- slice_tensors: bfloat16 [4, 2, 4, 2, 512, 256], P('cuts', None, 'bita', 'bitb'), may hold values from -4 to 4
- slice_gates: bfloat16 [4, 2, 2, 256, 256], P('cuts'), may hold values from -0.25 to 0.25
- last_gate: bfloat16 [2, 256, 256], replicated, may hold values from -0.25 to 0.25
- mix_first: float32 [2, 4, 4], replicated, may hold values from -2 to 2
- mix_second: float32 [2, 2, 2], replicated, may hold values from -3 to 3
- mix_joint: float32 [2, 8, 8], replicated, may hold values from -1.5 to 1.5
Outputs:
- amplitudes: float32 [2, 4, 2, 8, 64, 256], P(None, 'bita', 'bitb', None, 'cuts')
All inputs are finite; a program needn't handle non-finite values.
Results may differ from a plain program's by a relative error of at most 0.013.
Values may be sent and summed in bfloat16 or wider, within the bound.
A program may use at most 64 MiB of HBM per device.

v0:
```python
import jax
import jax.numpy as jnp
from jax import lax
from jax.sharding import PartitionSpec as P


def mix_group(values, matrix):
    return jnp.einsum("...csm,cd->...dsm", values, matrix, precision=lax.Precision.HIGHEST)


def contract(tensor, gate_pair, mixing):
    products = jnp.einsum(
        "z...k,wkm->zw...m", tensor, gate_pair, preferred_element_type=jnp.float32
    )
    real_part = products[0, 0] - products[1, 1]
    imag_part = products[0, 1] + products[1, 0]
    out_real = mix_group(real_part, mixing[0]) - mix_group(imag_part, mixing[1])
    out_imag = mix_group(real_part, mixing[1]) + mix_group(imag_part, mixing[0])
    return jnp.stack([out_real, out_imag])


def on_device(slice_tensors, slice_gates, last_gate, mix_first, mix_second, mix_joint):
    row_count = slice_tensors.shape[4]
    width_k = slice_tensors.shape[5]
    bita_size = lax.axis_size("bita")
    bitb_size = lax.axis_size("bitb")
    joint_size = bita_size * bitb_size
    own_gates = slice_gates[0]
    tensor = slice_tensors.reshape(2, bita_size, row_count // bita_size, width_k)
    tensor = lax.all_to_all(tensor, "bita", split_axis=1, concat_axis=1, tiled=True)
    tensor = contract(tensor, own_gates[0], mix_first).astype(jnp.bfloat16)
    tensor = tensor.reshape(2, bitb_size, row_count // bitb_size, width_k)
    tensor = lax.all_to_all(tensor, "bitb", split_axis=1, concat_axis=1, tiled=True)
    tensor = contract(tensor, own_gates[1], mix_second).astype(jnp.bfloat16)
    tensor = lax.all_to_all(
        tensor.reshape(2, joint_size, row_count // joint_size, width_k),
        ("bita", "bitb"),
        split_axis=1,
        concat_axis=1,
        tiled=True,
    )
    result = contract(tensor, last_gate, mix_joint)
    amplitudes = lax.psum_scatter(result, "cuts", scatter_dimension=2, tiled=True)
    return amplitudes.reshape(2, 1, 1, joint_size, amplitudes.shape[2], width_k)


def solution(mesh):
    placed = (
        P("cuts", None, "bita", "bitb", None, None),
        P("cuts", None, None, None, None),
        P(),
        P(),
        P(),
        P(),
    )
    return jax.shard_map(
        on_device,
        mesh=mesh,
        in_specs=placed,
        out_specs=P(None, "bita", "bitb", None, "cuts", None),
        check_vma=False,
    )
```

profile of v0, /device:TPU:0, one launch (start us, length us, event | category | flops | bytes accessed | tf_op | source)
XLA Modules:
  0.0 109.4 jit_solution(618267373609430234)
XLA Ops:
  6.5 0.0 copy-start
  6.5 0.0 copy-start.1
  6.5 0.0 reduce-scatter.5.cloned.1.call-start
  6.5 1.1 %copy.99 = bf16[2,4,128,256]{3,2,0,1:T(8,128)(2,1)S(1)} copy(bf16[2,4,128,256]{3,2,1,0:T(8,128)(2,1)} %bitcast.145) | data formatting | bytes 1048576 | tf_op jit(solution)/shard_map/reshape | solution.py:29
  7.7 20.6 %all_to_all.15 = bf16[2,4,128,256]{3,2,0,1:T(8,128)(2,1)S(1)} all-to-all(bf16[2,4,128,256]{3,2,0,1:T(8,128)(2,1)S(1)} %copy.99), channel_id=1, replica_groups=mesh['cuts'=4,'bita'=4,'bitb'=2] {'bita'}, dimensions={1} | all-to-all | bytes 1048576 | tf_op jit(solution)/shard_map/all_to_all | solution.py:30
  28.3 0.0 copy-done.1
  28.3 0.5 convolution_bitcast_fusion.2
  28.8 0.0 copy-start.3
  28.8 0.1 fusion.14
  28.9 0.2 copy.101
  29.2 0.3 copy-done.3
  29.5 1.0 fusion.45
  30.5 1.0 fusion.49
  31.6 0.2 copy.103
  31.8 1.1 fusion.8
  32.9 1.1 fusion.9
  34.0 0.1 pad_maximum_fusion.1
  34.1 9.5 %all_to_all.16 = bf16[2,2,256,256]{3,2,0,1:T(8,128)(2,1)S(1)} all-to-all(bf16[2,2,256,256]{3,2,0,1:T(8,128)(2,1)S(1)} %copy.111), channel_id=1, replica_groups=mesh['cuts'=4,'bita'=4,'bitb'=2] {'bitb'}, dimensions={1} | all-to-all | bytes 1048576 | tf_op jit(solution)/shard_map/all_to_all | solution.py:33
  43.6 0.4 convolution_bitcast_fusion.1
  44.1 0.0 copy-start.4
  44.1 0.1 fusion.12
  44.2 0.5 copy-done.4
  44.8 2.1 %fusion.28 = f32[256,256,2]{1,2,0:T(2,128)S(1)} fusion(f32[2,256,256]{2,1,0:T(8,128)S(1)} %get-tuple-element.8, f32[2,2,2]{2,1,0:T(2,128)S(1)} %copy-done.4), kind=kOutput, calls=%fused_computation.46 | convolution fusion | flops 3145728 | bytes 1049600 | tf_op jit(solution)/shard_map/...csm,cd->...dsm/dot_general | solution.py:8
  46.9 2.1 %fusion.30 = f32[256,256,2]{1,2,0:T(2,128)S(1)} fusion(f32[2,256,256]{2,1,0:T(8,128)S(1)} %get-tuple-element.8, f32[2,2,2]{2,1,0:T(2,128)S(1)} %copy-done.4), kind=kOutput, calls=%fused_computation.48 | convolution fusion | flops 3145728 | bytes 1049600 | tf_op jit(solution)/shard_map/...csm,cd->...dsm/dot_general | solution.py:8
  49.0 2.2 %fusion.6 = bf16[2,256,256]{2,0,1:T(2,128)(2,1)S(1)} fusion(f32[256,256,2]{1,2,0:T(2,128)S(1)} %fusion.28, f32[2,256,256]{2,1,0:T(8,128)S(1)} %get-tuple-element.7, f32[2,2,2]{2,1,0:T(2,128)S(1)} %copy-done.4), kind=kOutput, calls=%fused_computation.15 | convolution fusion | flops 3407872 | bytes 1311744 | tf_op jit(solution)/shard_map/...csm,cd->...dsm/dot_general | solution.py:8
  51.2 2.2 %fusion.7 = bf16[2,256,256]{2,0,1:T(2,128)(2,1)S(1)} fusion(f32[256,256,2]{1,2,0:T(2,128)S(1)} %fusion.30, f32[2,256,256]{2,1,0:T(8,128)S(1)} %get-tuple-element.7, f32[2,2,2]{2,1,0:T(2,128)S(1)} %copy-done.4), kind=kOutput, calls=%fused_computation.16 | convolution fusion | flops 3407872 | bytes 1311744 | tf_op jit(solution)/shard_map/...csm,cd->...dsm/dot_general | solution.py:8
  53.4 0.1 pad_maximum_fusion.2
  53.5 16.5 %all_to_all.17 = bf16[2,8,64,256]{3,2,0,1:T(8,128)(2,1)S(1)} all-to-all(bf16[2,8,64,256]{3,2,0,1:T(8,128)(2,1)S(1)} %copy.123), channel_id=1, replica_groups=mesh['cuts'=4,'bita'=4,'bitb'=2] {'bita','bitb'}, dimensions={1} | all-to-all | bytes 1048576 | tf_op jit(solution)/shard_map/all_to_all | solution.py:35
  70.0 0.0 copy-done
  70.0 0.4 convolution_bitcast_fusion
  70.5 0.0 copy-start.2
  70.5 0.2 fusion.10
  70.6 0.5 copy-done.2
  71.2 0.9 fusion.22
  72.0 0.9 fusion.24
  72.9 0.9 fusion.1
  73.8 0.9 fusion
  74.7 0.1 pad_maximum_fusion
  74.8 0.1 copy.167
  74.9 1.6 %copy.170 = f32[8,8,16,256]{3,1,2,0:T(8,128)} copy(f32[8,8,16,256]{3,2,1,0:T(8,128)S(1)} %bitcast.138) | data formatting | bytes 2097152
  76.5 0.0 reduce-scatter.5.cloned.1.call-update
  76.6 24.1 %reduce-scatter.5.cloned.1.call-done = f32[16,4096]{1,0:T(8,128)} async-done(((f32[64,4096]{1,0:T(8,128)}), f32[16,4096]{1,0:T(8,128)}) %reduce-scatter.5.cloned.1.call-update) | async-done | bytes 262160
  100.7 1.0 copy.171
  101.7 0.8 copy.133
  (7 shorter events, 0.2 us)
Async XLA Ops:
  6.5 63.5 %copy-start = (bf16[2,256,256]{2,1,0:T(8,128)(2,1)S(1)}, bf16[2,256,256]{2,1,0:T(8,128)(2,1)}, u32[]{:S(2)}) copy-start(bf16[2,256,256]{2,1,0:T(8,128)(2,1)} %param.8) | copy-start | bytes 786436
  6.5 21.8 %copy-start.1 = (bf16[1,2,2,256,256]{4,3,2,1,0:T(8,128)(2,1)S(1)}, bf16[1,2,2,256,256]{4,3,2,1,0:T(8,128)(2,1)}, u32[]{:S(2)}) copy-start(bf16[1,2,2,256,256]{4,3,2,1,0:T(8,128)(2,1)} %param.7) | copy-start | bytes 1572868
  6.5 94.1 %reduce-scatter.5.cloned.1.call-start = ((), (), s32[]{:S(2)}) async-start(), calls=%async_computation.4 | async-start | bytes 1310720
  28.8 0.7 copy-start.3
  44.1 0.7 copy-start.4
  70.5 0.7 copy-start.2
Sparse Core Ops, SparseCore 0:
  76.7 23.9 reduce-scatter.4
where the time goes:
time: 110 us; the launch traced here: 109 us
  blocking collectives  46.6 us (42%)
  waiting for transfers between devices  24.1 us (22%)
  matrix products  17.6 us (16%)
  between operations  13.6 us (12%)
  local copies, waits for them, and re-layouts  6.76 us (6%)
    unnamed x2, waiting for transfers between devices  24.1 us
    all_to_all x1, blocking collectives, on_device(): lax.all_to_all(tensor, 'bita', split_axis=1, concat_axis=1, tiled=True)  20.6 us
    all_to_all x1, blocking collectives, on_device(): lax.all_to_all(tensor.reshape(2, joint_size, row_count // joint_size, wid...  16.5 us
    dot_general x12, matrix products, mix_group(): jnp.einsum('...csm,cd->...dsm', values, matrix, precision=lax.Precision.H...  16.3 us
    all_to_all x1, blocking collectives, on_device(): lax.all_to_all(tensor, 'bitb', split_axis=1, concat_axis=1, tiled=True)  9.53 us
    unnamed x14, local copies, waits for them, and re-layouts  4.17 us
  transfers between devices with their start and end apart: 1, of which 1 were waited for; matrix products, arithmetic and copies ran while one was open for 0% of the time, Pallas kernels for 0%

commit v1 on v0

--- a/solution.py
+++ b/solution.py
@@ -1,7 +1,15 @@
+import functools
+
 import jax
 import jax.numpy as jnp
 from jax import lax
+from jax.experimental import pallas as pl
+from jax.experimental.pallas import tpu as pltpu
 from jax.sharding import PartitionSpec as P
+
+MESH = pl.DeviceIdType.MESH
+BF16 = jnp.bfloat16
+F32 = jnp.float32
 
 
 def mix_group(values, matrix):
@@ -19,7 +27,7 @@
     return jnp.stack([out_real, out_imag])
 
 
-def on_device(slice_tensors, slice_gates, last_gate, mix_first, mix_second, mix_joint):
+def by_collectives(slice_tensors, slice_gates, last_gate, mix_first, mix_second, mix_joint):
     row_count = slice_tensors.shape[4]
     width_k = slice_tensors.shape[5]
     bita_size = lax.axis_size("bita")
@@ -44,6 +52,196 @@
     return amplitudes.reshape(2, 1, 1, joint_size, amplitudes.shape[2], width_k)
 
 
+def dot(a, b):
+    return jnp.dot(a, b, preferred_element_type=F32)
+
+
+def wide(real, imag):
+    return (
+        jnp.concatenate([real, imag], axis=1),
+        jnp.concatenate([-imag, real], axis=1),
+    )
+
+
+def kernel(
+    x_ref, gates_ref, last_ref, m1_ref, m2_ref, mj_ref, out_ref,
+    send_a, recv_a, send_b, recv_b, send_c, recv_c, send_d, recv_d,
+    a_send_sem, a_recv_sem, b_send_sem, b_recv_sem,
+    c_send_sem, c_recv_sem, d_send_sem, d_recv_sem,
+):
+    cut = lax.axis_index("cuts")
+    bita = lax.axis_index("bita")
+    bitb = lax.axis_index("bitb")
+    na, nb = 4, 2
+    width = x_ref.shape[5]
+    rows = x_ref.shape[4]
+    fine = out_ref.shape[4]
+    y, core = cut // 2, lax.rem(cut, 2)
+    at_core = y * 2 + (1 - core)
+    at_y = (1 - y) * 2 + core
+    to_core = (at_core, bita, bitb)
+    to_y = (at_y, bita, bitb)
+    to_x = (cut, bita, 1 - bitb)
+    to_z = [(cut, lax.rem(bita + d, na), bitb) for d in range(1, na)]
+
+    barrier = pltpu.get_barrier_semaphore()
+    for device in [to_core, to_y, to_x] + to_z:
+        pl.semaphore_signal(barrier, inc=1, device_id=device, device_id_type=MESH)
+
+    g1 = wide(gates_ref[0, 1, 0], gates_ref[0, 1, 1])
+    both = dot(gates_ref[0, 0, 0], g1[0]) + dot(gates_ref[0, 0, 1], g1[1])
+    both = both.astype(BF16)
+    gate = wide(both[:, :width], both[:, width:])
+
+    def product(target, halves):
+        parts = []
+        for z in range(2):
+            pieces = []
+            for half in halves:
+                for u in range(na):
+                    start = u * (rows // na) + half * (rows // na // nb) + target * fine
+                    pieces.append(x_ref[0, z, 0, 0, pl.ds(pl.multiple_of(start, 16), fine), :])
+            parts.append(jnp.concatenate(pieces, axis=0))
+        return dot(parts[0], gate[0]) + dot(parts[1], gate[1])
+
+    halves = (1 - bitb, bitb)
+    part = na * fine
+
+    def remote(src, dst, send_sem, recv_sem, device):
+        return pltpu.make_async_remote_copy(
+            src_ref=src, dst_ref=dst, send_sem=send_sem, recv_sem=recv_sem,
+            device_id=device, device_id_type=MESH,
+        )
+
+    a_copies, b_copies, d_copies = [], [], []
+    for i, target in enumerate(((1 - y) * 2 + (1 - core), y * 2 + (1 - core))):
+        send_a[i] = product(target, halves).astype(BF16)
+        if i == 0:
+            pl.semaphore_wait(barrier, 6)
+        copy = remote(send_a.at[i], recv_a.at[i], a_send_sem.at[i], a_recv_sem.at[i], to_core)
+        copy.start()
+        a_copies.append(copy)
+
+    total = product(at_y, halves)
+    a_copies[0].wait_recv()
+    for q in range(nb):
+        rows_q = slice(q * part, (q + 1) * part)
+        send_b[q] = (total[rows_q] + recv_a[0, rows_q].astype(F32)).astype(BF16)
+        copy = remote(send_b.at[q], recv_b.at[q], b_send_sem.at[q], b_recv_sem.at[q], to_y)
+        copy.start()
+        b_copies.append(copy)
+    total = product(cut, halves)
+    a_copies[1].wait_recv()
+    total = total + recv_a[1].astype(F32)
+
+    b_copies[0].wait_recv()
+    send_c[...] = (total[:part] + recv_b[0].astype(F32)).astype(BF16)
+    c_copy = remote(send_c, recv_c, c_send_sem.at[0], c_recv_sem.at[0], to_x)
+    c_copy.start()
+
+    low = lax.rem(bita, 2)
+    lanes = na * na * fine
+    w_id = lax.broadcasted_iota(jnp.int32, (na * nb, lanes), 0)
+    lane = lax.broadcasted_iota(jnp.int32, (na * nb, lanes), 1)
+    u_id = lax.rem(lane // fine, na)
+    d_id = lane // (fine * na)
+    mixed = [jnp.zeros((na * nb, lanes), F32), jnp.zeros((na * nb, lanes), F32)]
+    for b in range(nb):
+        first, joint = [], []
+        for z in range(2):
+            a_part = jnp.zeros((na * nb, lanes), F32)
+            for d in range(na):
+                a_part = jnp.where(d_id == d, m1_ref[z, lax.rem(bita + d, na), b * 2 + low], a_part)
+            j_part = jnp.zeros((na * nb, lanes), F32)
+            for u in range(na):
+                for w in range(na * nb):
+                    j_part = jnp.where((u_id == u) & (w_id == w), mj_ref[z, u * nb + b, w], j_part)
+            first.append(a_part)
+            joint.append(j_part)
+        mixed[0] += first[0] * joint[0] - first[1] * joint[1]
+        mixed[1] += first[0] * joint[1] + first[1] * joint[0]
+    same = lax.rem(
+        lax.broadcasted_iota(jnp.int32, (fine, lanes), 1), fine
+    ) == lax.broadcasted_iota(jnp.int32, (fine, lanes), 0)
+    spread = []
+    for z in range(2):
+        spread.append(jnp.concatenate(
+            [jnp.where(same, mixed[z][w:w + 1], 0.0) for w in range(na * nb)], axis=0
+        ).astype(BF16))
+    last = wide(last_ref[0], last_ref[1])
+
+    b_copies[1].wait_recv()
+    own = total[part:] + recv_b[1].astype(F32)
+    own_r, own_i = own[:, :width], own[:, width:]
+    c_copy.wait_recv()
+    other = recv_c[...].astype(F32)
+    other_r, other_i = other[:, :width], other[:, width:]
+    for v in range(nb):
+        kr, ki = m2_ref[0, bitb, v], m2_ref[1, bitb, v]
+        pr, pi = m2_ref[0, 1 - bitb, v], m2_ref[1, 1 - bitb, v]
+        send_d[v] = jnp.concatenate([
+            own_r * kr - own_i * ki + other_r * pr - other_i * pi,
+            own_r * ki + own_i * kr + other_r * pi + other_i * pr,
+        ], axis=1).astype(BF16)
+    for d in range(1, na):
+        to = lax.rem(bita + d, na)
+        copy = remote(
+            send_d.at[to // 2], recv_d.at[na - 1 - d], d_send_sem.at[d - 1],
+            d_recv_sem.at[na - 1 - d], (cut, to, bitb),
+        )
+        copy.start()
+        d_copies.append(copy)
+
+    def piece(s, value):
+        columns = slice(s * part, (s + 1) * part)
+        return dot(spread[0][:, columns], value), dot(spread[1][:, columns], value)
+
+    sum_r, sum_i = piece(0, send_d[bita // 2])
+    for s in range(1, na):
+        d_copies[na - 1 - s].wait_recv()
+        more = piece(s, recv_d[s - 1])
+        sum_r += more[0]
+        sum_i += more[1]
+    real = (sum_r[:, :width] - sum_i[:, width:]).astype(BF16)
+    imag = (sum_r[:, width:] + sum_i[:, :width]).astype(BF16)
+    result = dot(real, last[0]) + dot(imag, last[1])
+    for z in range(2):
+        out_ref[z, 0, 0] = result[:, z * width:(z + 1) * width].reshape(na * nb, fine, width)
+    for copy in a_copies + b_copies + [c_copy] + d_copies:
+        copy.wait_send()
+
+
+def by_kernel(slice_tensors, slice_gates, last_gate, mix_first, mix_second, mix_joint):
+    rows, width = slice_tensors.shape[4:]
+    na, nb, cuts = lax.axis_size("bita"), lax.axis_size("bitb"), lax.axis_size("cuts")
+    fine = rows // (na * nb * cuts)
+    part = na * fine
+    vmem = pl.BlockSpec(memory_space=pltpu.VMEM)
+    smem = pl.BlockSpec(memory_space=pltpu.SMEM)
+    dma = pltpu.SemaphoreType.DMA
+    return pl.pallas_call(
+        kernel,
+        out_shape=jax.ShapeDtypeStruct((2, 1, 1, na * nb, fine, width), F32),
+        in_specs=[vmem] * 3 + [smem] * 3,
+        out_specs=vmem,
+        scratch_shapes=[
+            pltpu.VMEM((2, nb * part, 2 * width), BF16),
+            pltpu.VMEM((2, nb * part, 2 * width), BF16),
+            pltpu.VMEM((nb, part, 2 * width), BF16),
+            pltpu.VMEM((nb, part, 2 * width), BF16),
+            pltpu.VMEM((part, 2 * width), BF16),
+            pltpu.VMEM((part, 2 * width), BF16),
+            pltpu.VMEM((nb, part, 2 * width), BF16),
+            pltpu.VMEM((na - 1, part, 2 * width), BF16),
+            dma((2,)), dma((2,)), dma((2,)), dma((2,)),
+            dma((1,)), dma((1,)), dma((na - 1,)), dma((na - 1,)),
+        ],
+        compiler_params=pltpu.CompilerParams(
+            collective_id=0, has_side_effects=True, vmem_limit_bytes=32 * 2**20
+        ),
+    )(slice_tensors, slice_gates, last_gate, mix_first, mix_second, mix_joint)
+
+
 def solution(mesh):
     placed = (
         P("cuts", None, "bita", "bitb", None, None),
@@ -53,8 +251,9 @@
         P(),
         P(),
     )
+    pairs = (mesh.shape["cuts"], mesh.shape["bita"], mesh.shape["bitb"]) == (4, 4, 2)
     return jax.shard_map(
-        on_device,
+        by_kernel if pairs else by_collectives,
         mesh=mesh,
         in_specs=placed,
         out_specs=P(None, "bita", "bitb", None, "cuts", None),

time: 110 us -> 26.9 us (0.24)
  blocking collectives: 46.6 us -> 0 us
  waiting for transfers between devices: 24.1 us -> 0 us
  Pallas kernels: 0 us -> 20.7 us
  matrix products: 17.6 us -> 0 us
  between operations: 13.6 us -> 0.02 us
    all_to_all x3 -> x0, blocking collectives: 46.6 us -> none  [the longest x1 20.6 us: on_device(): lax.all_to_all(tensor, 'bita', split_axis=1, concat_axis=1, tiled=True)]
    unnamed x2 -> x0, waiting for transfers between devices: 24.1 us -> none
    pallas_call x0 -> x1, Pallas kernels: none -> 20.7 us  [by_kernel(): pl.pallas_call(kernel, out_shape=jax.ShapeDtypeStruct((2, 1, 1, na * nb,...]
    dot_general x15 -> x0, matrix products: 17.6 us -> none  [the longest x12 16.3 us: mix_group(): jnp.einsum('...csm,cd->...dsm', values, matrix, precision=lax.Precision.H...]
    reshape x2 -> x0, local copies, waits for them, and re-layouts: 1.93 us -> none  [the longest x1 1.15 us: on_device(): slice_tensors.reshape(2, bita_size, row_count // bita_size, width_k)]
    unnamed x14 -> x13, local copies, waits for them, and re-layouts: 4.17 us -> 5.8 us
  transfers between devices with their start and end apart: 1 -> 0, of which waited for: 1 -> 0; matrix products, arithmetic and copies ran while one was open for 0% -> 0% of each run, Pallas kernels for 0% -> 0%
where the time goes in v1:
time: 26.9 us; the launch traced here: 26.5 us
  Pallas kernels  20.7 us (77%)
  local copies, waits for them, and re-layouts  5.8 us (22%)
    pallas_call x1, Pallas kernels, by_kernel(): pl.pallas_call(kernel, out_shape=jax.ShapeDtypeStruct((2, 1, 1, na * nb,...  20.7 us
    unnamed x13, local copies, waits for them, and re-layouts  5.8 us

profile of v1, /device:TPU:0, one launch (start us, length us, event | category | flops | bytes accessed | tf_op | source)
XLA Modules:
  0.0 26.5 jit_solution(6926828138636824838)
XLA Ops:
  0.0 0.0 copy-start
  0.0 1.0 %copy-done = bf16[1,2,1,1,512,256]{5,4,3,2,1,0:T(8,128)(2,1)S(1)} copy-done((bf16[1,2,1,1,512,256]{5,4,3,2,1,0:T(8,128)(2,1)S(1)}, bf16[1,2,1,1,512,256]{5,4,3,2,1,0:T(8,128)(2,1)}, u32[]{:S(2)}) %copy-start) | copy-done | bytes 524312
  1.0 0.0 copy-start.1
  1.0 1.0 %copy-done.1 = bf16[1,2,2,256,256]{4,3,2,1,0:T(8,128)(2,1)S(1)} copy-done((bf16[1,2,2,256,256]{4,3,2,1,0:T(8,128)(2,1)S(1)}, bf16[1,2,2,256,256]{4,3,2,1,0:T(8,128)(2,1)}, u32[]{:S(2)}) %copy-start.1) | copy-done | bytes 524312
  2.1 0.0 copy-start.2
  2.1 0.9 %copy-done.2 = bf16[2,256,256]{2,1,0:T(8,128)(2,1)S(1)} copy-done((bf16[2,256,256]{2,1,0:T(8,128)(2,1)S(1)}, bf16[2,256,256]{2,1,0:T(8,128)(2,1)}, u32[]{:S(2)}) %copy-start.2) | copy-done | bytes 262168
  3.0 0.0 copy-start.3
  3.0 0.7 %copy-done.3 = f32[2,8,8]{2,1,0:T(8,128)S(1)} copy-done((f32[2,8,8]{2,1,0:T(8,128)S(1)}, f32[2,8,8]{2,1,0:T(8,128)}, u32[]{:S(2)}) %copy-start.3) | copy-done | bytes 536
  3.7 0.0 copy-start.4
  3.7 0.7 %copy-done.4 = f32[2,4,4]{2,1,0:T(4,128)S(1)} copy-done((f32[2,4,4]{2,1,0:T(4,128)S(1)}, f32[2,4,4]{2,1,0:T(4,128)}, u32[]{:S(2)}) %copy-start.4) | copy-done | bytes 152
  4.4 0.0 copy-start.5
  4.4 0.7 %copy-done.5 = f32[2,2,2]{2,1,0:T(2,128)S(1)} copy-done((f32[2,2,2]{2,1,0:T(2,128)S(1)}, f32[2,2,2]{2,1,0:T(2,128)}, u32[]{:S(2)}) %copy-start.5) | copy-done | bytes 56
  5.1 20.7 %shard_map.64 = f32[2,1,1,8,16,256]{5,4,3,2,1,0:T(8,128)S(1)} custom-call(bf16[1,2,1,1,512,256]{5,4,3,2,1,0:T(8,128)(2,1)S(1)} %copy-done, bf16[1,2,2,256,256]{4,3,2,1,0:T(8,128)(2,1)S(1)} %copy-done.1, bf16[2,256,256]{2,1,0:T(8,128)(2,1)S(1)} %copy-done.2, f32[2,4,4]{2,1,0:T(4,128)S(1)} %copy-done.4, f32[2,2,2]{2,1,0:T(2,128)S(1)} %copy-done.5, ...), custom_call_target="tpu_custom_call" | custom-call | tf_op jit(solution)/shard_map/pallas_call | solution.py:222
  25.8 0.7 %copy.8 = f32[2,1,1,8,16,256]{5,4,3,2,1,0:T(8,128)} copy(f32[2,1,1,8,16,256]{5,4,3,2,1,0:T(8,128)S(1)} %shard_map.64) | data formatting | bytes 524288
Async XLA Ops:
  0.0 1.0 %copy-start = (bf16[1,2,1,1,512,256]{5,4,3,2,1,0:T(8,128)(2,1)S(1)}, bf16[1,2,1,1,512,256]{5,4,3,2,1,0:T(8,128)(2,1)}, u32[]{:S(2)}) copy-start(bf16[1,2,1,1,512,256]{5,4,3,2,1,0:T(8,128)(2,1)} %x_ref.1) | copy-start | bytes 1572868
  1.0 1.0 %copy-start.1 = (bf16[1,2,2,256,256]{4,3,2,1,0:T(8,128)(2,1)S(1)}, bf16[1,2,2,256,256]{4,3,2,1,0:T(8,128)(2,1)}, u32[]{:S(2)}) copy-start(bf16[1,2,2,256,256]{4,3,2,1,0:T(8,128)(2,1)} %gates_ref.1) | copy-start | bytes 1572868
  2.1 0.9 %copy-start.2 = (bf16[2,256,256]{2,1,0:T(8,128)(2,1)S(1)}, bf16[2,256,256]{2,1,0:T(8,128)(2,1)}, u32[]{:S(2)}) copy-start(bf16[2,256,256]{2,1,0:T(8,128)(2,1)} %last_ref.1) | copy-start | bytes 786436
  3.0 0.7 %copy-start.3 = (f32[2,8,8]{2,1,0:T(8,128)S(1)}, f32[2,8,8]{2,1,0:T(8,128)}, u32[]{:S(2)}) copy-start(f32[2,8,8]{2,1,0:T(8,128)} %mj_ref.1) | copy-start | bytes 1540
  3.7 0.7 %copy-start.4 = (f32[2,4,4]{2,1,0:T(4,128)S(1)}, f32[2,4,4]{2,1,0:T(4,128)}, u32[]{:S(2)}) copy-start(f32[2,4,4]{2,1,0:T(4,128)} %m1_ref.1) | copy-start | bytes 388
  4.4 0.7 %copy-start.5 = (f32[2,2,2]{2,1,0:T(2,128)S(1)}, f32[2,2,2]{2,1,0:T(2,128)}, u32[]{:S(2)}) copy-start(f32[2,2,2]{2,1,0:T(2,128)} %m2_ref.1) | copy-start | bytes 100

commit v2 on v1

v2 whole, which is shorter than its diff:
```python
import functools

import jax
import jax.numpy as jnp
from jax import lax
from jax.experimental import pallas as pl
from jax.experimental.pallas import tpu as pltpu
from jax.sharding import PartitionSpec as P

MESH = pl.DeviceIdType.MESH
BF16 = jnp.bfloat16
F32 = jnp.float32


def mix_group(values, matrix):
    return jnp.einsum("...csm,cd->...dsm", values, matrix, precision=lax.Precision.HIGHEST)


def contract(tensor, gate_pair, mixing):
    products = jnp.einsum(
        "z...k,wkm->zw...m", tensor, gate_pair, preferred_element_type=jnp.float32
    )
    real_part = products[0, 0] - products[1, 1]
    imag_part = products[0, 1] + products[1, 0]
    out_real = mix_group(real_part, mixing[0]) - mix_group(imag_part, mixing[1])
    out_imag = mix_group(real_part, mixing[1]) + mix_group(imag_part, mixing[0])
    return jnp.stack([out_real, out_imag])


def by_collectives(slice_tensors, slice_gates, last_gate, mix_first, mix_second, mix_joint):
    row_count = slice_tensors.shape[4]
    width_k = slice_tensors.shape[5]
    bita_size = lax.axis_size("bita")
    bitb_size = lax.axis_size("bitb")
    joint_size = bita_size * bitb_size
    own_gates = slice_gates[0]
    tensor = slice_tensors.reshape(2, bita_size, row_count // bita_size, width_k)
    tensor = lax.all_to_all(tensor, "bita", split_axis=1, concat_axis=1, tiled=True)
    tensor = contract(tensor, own_gates[0], mix_first).astype(jnp.bfloat16)
    tensor = tensor.reshape(2, bitb_size, row_count // bitb_size, width_k)
    tensor = lax.all_to_all(tensor, "bitb", split_axis=1, concat_axis=1, tiled=True)
    tensor = contract(tensor, own_gates[1], mix_second).astype(jnp.bfloat16)
    tensor = lax.all_to_all(
        tensor.reshape(2, joint_size, row_count // joint_size, width_k),
        ("bita", "bitb"),
        split_axis=1,
        concat_axis=1,
        tiled=True,
    )
    result = contract(tensor, last_gate, mix_joint)
    amplitudes = lax.psum_scatter(result, "cuts", scatter_dimension=2, tiled=True)
    return amplitudes.reshape(2, 1, 1, joint_size, amplitudes.shape[2], width_k)


def dot(a, b):
    return jnp.dot(a, b, preferred_element_type=F32)


def wide(real, imag):
    return (
        jnp.concatenate([real, imag], axis=1),
        jnp.concatenate([-imag, real], axis=1),
    )


def kernel(
    x_hbm, gates_hbm, last_hbm, m1_hbm, m2_hbm, mj_hbm, out_ref,
    x_ref, gates_ref, last_ref, m1_ref, m2_ref, mj_ref,
    send_a, recv_a, send_b, recv_b, send_c, recv_c, send_d, recv_d,
    load_sem, a_send_sem, a_recv_sem, b_send_sem, b_recv_sem,
    c_send_sem, c_recv_sem, d_send_sem, d_recv_sem,
):
    cut = lax.axis_index("cuts")
    bita = lax.axis_index("bita")
    bitb = lax.axis_index("bitb")
    na, nb = 4, 2
    _, rows, width = x_ref.shape
    fine = out_ref.shape[4]
    y, core = cut // 2, lax.rem(cut, 2)
    at_core = y * 2 + (1 - core)
    at_y = (1 - y) * 2 + core
    to_core = (at_core, bita, bitb)
    to_y = (at_y, bita, bitb)
    to_x = (cut, bita, 1 - bitb)
    to_z = [(cut, lax.rem(bita + d, na), bitb) for d in range(1, na)]

    def load(src, dst, i):
        copy = pltpu.make_async_copy(src, dst, load_sem.at[i])
        copy.start()
        return copy

    load_gates = [load(gates_hbm.at[0, i], gates_ref.at[i], i) for i in (1, 0)]
    load_x = [load(x_hbm.at[0, z, 0, 0], x_ref.at[z], 2 + z) for z in range(2)]
    load_rest = [
        load(src, dst, 4 + i)
        for i, (src, dst) in enumerate((
            (m1_hbm, m1_ref), (m2_hbm, m2_ref), (mj_hbm, mj_ref), (last_hbm, last_ref)
        ))
    ]

    barrier = pltpu.get_barrier_semaphore()
    for device in [to_core, to_y, to_x] + to_z:
        pl.semaphore_signal(barrier, inc=1, device_id=device, device_id_type=MESH)

    for copy in load_gates:
        copy.wait()
    g1 = wide(gates_ref[1, 0], gates_ref[1, 1])
    both = dot(gates_ref[0, 0], g1[0]) + dot(gates_ref[0, 1], g1[1])
    both = both.astype(BF16)
    gate = wide(both[:, :width], both[:, width:])
    for copy in load_x:
        copy.wait()

    chunks = ((0, 2), (1, 3))
    halves = (1 - bitb, bitb)
    part = 2 * fine

    def product(target):
        parts = []
        for z in range(2):
            pieces = []
            for half in halves:
                for chunk in chunks:
                    for u in chunk:
                        start = u * (rows // na) + half * (rows // na // nb) + target * fine
                        pieces.append(x_ref[z, pl.ds(pl.multiple_of(start, 16), fine), :])
            parts.append(jnp.concatenate(pieces, axis=0))
        return dot(parts[0], gate[0]) + dot(parts[1], gate[1])

    def remote(src, dst, send_sem, recv_sem, device):
        return pltpu.make_async_remote_copy(
            src_ref=src, dst_ref=dst, send_sem=send_sem, recv_sem=recv_sem,
            device_id=device, device_id_type=MESH,
        )

    a_copies, b_copies, c_copies, d_copies = [], [], [], []
    for i, target in enumerate(((1 - y) * 2 + (1 - core), y * 2 + (1 - core))):
        send_a[i] = product(target).astype(BF16)
        if i == 0:
            pl.semaphore_wait(barrier, 6)
        copy = remote(send_a.at[i], recv_a.at[i], a_send_sem.at[i], a_recv_sem.at[i], to_core)
        copy.start()
        a_copies.append(copy)

    total = product(at_y)
    a_copies[0].wait_recv()
    for q in range(4):
        rows_q = slice(q * part, (q + 1) * part)
        send_b[q] = (total[rows_q] + recv_a[0, rows_q].astype(F32)).astype(BF16)
        copy = remote(send_b.at[q], recv_b.at[q], b_send_sem.at[q], b_recv_sem.at[q], to_y)
        copy.start()
        b_copies.append(copy)
    total = product(cut)
    a_copies[1].wait_recv()
    total = total + recv_a[1].astype(F32)

    def summed(q):
        b_copies[q].wait_recv()
        return total[q * part:(q + 1) * part] + recv_b[q].astype(F32)

    for copy in load_rest:
        copy.wait()
    low = lax.rem(bita, 2)
    lanes = na * na * fine
    by_fine = fine.bit_length() - 1
    w_id = lax.broadcasted_iota(jnp.int32, (na * nb, lanes), 0)
    lane = lax.broadcasted_iota(jnp.int32, (na * nb, lanes), 1)
    u_id = (((lane >> by_fine) & 1) << 1) | (lane >> (by_fine + 3))
    d_id = (lane >> (by_fine + 1)) & 3
    mixed = [jnp.zeros((na * nb, lanes), F32), jnp.zeros((na * nb, lanes), F32)]
    for b in range(nb):
        first, joint = [], []
        for z in range(2):
            a_part = jnp.zeros((na * nb, lanes), F32)
            for d in range(na):
                a_part = jnp.where(d_id == d, m1_ref[z, lax.rem(bita + d, na), b * 2 + low], a_part)
            j_part = jnp.zeros((na * nb, lanes), F32)
            for u in range(na):
                for w in range(na * nb):
                    j_part = jnp.where((u_id == u) & (w_id == w), mj_ref[z, u * nb + b, w], j_part)
            first.append(a_part)
            joint.append(j_part)
        mixed[0] += first[0] * joint[0] - first[1] * joint[1]
        mixed[1] += first[0] * joint[1] + first[1] * joint[0]

    for h in range(2):
        send_c[h] = summed(h).astype(BF16)
        copy = remote(send_c.at[h], recv_c.at[h], c_send_sem.at[h], c_recv_sem.at[h], to_x)
        copy.start()
        c_copies.append(copy)

    same = (
        lax.broadcasted_iota(jnp.int32, (fine, lanes), 1) & (fine - 1)
    ) == lax.broadcasted_iota(jnp.int32, (fine, lanes), 0)
    spread = jnp.concatenate([
        jnp.where(same, mixed[z][w:w + 1], 0.0) for z in range(2) for w in range(na * nb)
    ], axis=0).astype(BF16)
    last = wide(last_ref[0], last_ref[1])

    for h in range(2):
        own = summed(2 + h)
        own_r, own_i = own[:, :width], own[:, width:]
        c_copies[h].wait_recv()
        other = recv_c[h].astype(F32)
        other_r, other_i = other[:, :width], other[:, width:]
        for v in range(nb):
            kr, ki = m2_ref[0, bitb, v], m2_ref[1, bitb, v]
            pr, pi = m2_ref[0, 1 - bitb, v], m2_ref[1, 1 - bitb, v]
            send_d[h, v] = jnp.concatenate([
                own_r * kr - own_i * ki + other_r * pr - other_i * pi,
                own_r * ki + own_i * kr + other_r * pi + other_i * pr,
            ], axis=1).astype(BF16)
        for d in (2, 1, 3):
            to = lax.rem(bita + d, na)
            copy = remote(
                send_d.at[h, to // 2], recv_d.at[h, na - 1 - d], d_send_sem.at[h, d - 1],
                d_recv_sem.at[h, na - 1 - d], (cut, to, bitb),
            )
            copy.start()
            d_copies.append(copy)

    columns = na * part
    sums = None
    for h in range(2):
        for copy in d_copies[h * (na - 1):(h + 1) * (na - 1)]:
            copy.wait_recv()
        value = jnp.concatenate(
            [send_d[h, bita // 2]] + [recv_d[h, s] for s in range(na - 1)], axis=0
        )
        more = dot(spread[:, h * columns:(h + 1) * columns], value)
        sums = more if sums is None else sums + more
    count = na * nb * fine
    real = (sums[:count, :width] - sums[count:, width:]).astype(BF16)
    imag = (sums[:count, width:] + sums[count:, :width]).astype(BF16)
    result = dot(real, last[0]) + dot(imag, last[1])
    for z in range(2):
        out_ref[z, 0, 0] = result[:, z * width:(z + 1) * width].reshape(na * nb, fine, width)
    for copy in a_copies + b_copies + c_copies + d_copies:
        copy.wait_send()


def by_kernel(slice_tensors, slice_gates, last_gate, mix_first, mix_second, mix_joint):
    rows, width = slice_tensors.shape[4:]
    na, nb, cuts = lax.axis_size("bita"), lax.axis_size("bitb"), lax.axis_size("cuts")
    fine = rows // (na * nb * cuts)
    part = 2 * fine
    hbm = pl.BlockSpec(memory_space=pltpu.MemorySpace.HBM)
    dma = pltpu.SemaphoreType.DMA
    return pl.pallas_call(
        kernel,
        out_shape=jax.ShapeDtypeStruct((2, 1, 1, na * nb, fine, width), F32),
        in_specs=[hbm] * 6,
        out_specs=pl.BlockSpec(memory_space=pltpu.VMEM),
        scratch_shapes=[
            pltpu.VMEM((2, rows, width), BF16),
            pltpu.VMEM(slice_gates.shape[1:], BF16),
            pltpu.VMEM(last_gate.shape, BF16),
            pltpu.SMEM(mix_first.shape, F32),
            pltpu.SMEM(mix_second.shape, F32),
            pltpu.SMEM(mix_joint.shape, F32),
            pltpu.VMEM((2, 4 * part, 2 * width), BF16),
            pltpu.VMEM((2, 4 * part, 2 * width), BF16),
            pltpu.VMEM((4, part, 2 * width), BF16),
            pltpu.VMEM((4, part, 2 * width), BF16),
            pltpu.VMEM((2, part, 2 * width), BF16),
            pltpu.VMEM((2, part, 2 * width), BF16),
            pltpu.VMEM((2, nb, part, 2 * width), BF16),
            pltpu.VMEM((2, na - 1, part, 2 * width), BF16),
            dma((8,)), dma((2,)), dma((2,)), dma((4,)), dma((4,)),
            dma((2,)), dma((2,)), dma((2, na - 1)), dma((2, na - 1)),
        ],
        compiler_params=pltpu.CompilerParams(
            collective_id=0, has_side_effects=True, vmem_limit_bytes=32 * 2**20
        ),
    )(slice_tensors, slice_gates, last_gate, mix_first, mix_second, mix_joint)


def solution(mesh):
    placed = (
        P("cuts", None, "bita", "bitb", None, None),
        P("cuts", None, None, None, None),
        P(),
        P(),
        P(),
        P(),
    )
    pairs = (mesh.shape["cuts"], mesh.shape["bita"], mesh.shape["bitb"]) == (4, 4, 2)
    return jax.shard_map(
        by_kernel if pairs else by_collectives,
        mesh=mesh,
        in_specs=placed,
        out_specs=P(None, "bita", "bitb", None, "cuts", None),
        check_vma=False,
    )
```

time: 26.9 us -> 26.1 us (0.970)
  Pallas kernels: 20.7 us -> 19.9 us
    pallas_call x1, Pallas kernels: 20.7 us -> 19.9 us  [by_kernel(): pl.pallas_call(kernel, out_shape=jax.ShapeDtypeStruct((2, 1, 1, na * nb,...]
where the time goes in v2:
time: 26.1 us; the launch traced here: 25.8 us
  Pallas kernels  19.9 us (76%)
  local copies, waits for them, and re-layouts  5.8 us (22%)
    pallas_call x1, Pallas kernels, by_kernel(): pl.pallas_call(kernel, out_shape=jax.ShapeDtypeStruct((2, 1, 1, na * nb,...  19.9 us
    unnamed x13, local copies, waits for them, and re-layouts  5.8 us

profile of v2, /device:TPU:0, one launch (start us, length us, event | category | flops | bytes accessed | tf_op | source)
XLA Modules:
  0.0 25.8 jit_solution(13429764462845304606)
XLA Ops:
  0.0 0.0 copy-start
  0.0 1.0 %copy-done = bf16[1,2,1,1,512,256]{5,4,3,2,1,0:T(8,128)(2,1)S(1)} copy-done((bf16[1,2,1,1,512,256]{5,4,3,2,1,0:T(8,128)(2,1)S(1)}, bf16[1,2,1,1,512,256]{5,4,3,2,1,0:T(8,128)(2,1)}, u32[]{:S(2)}) %copy-start) | copy-done | bytes 524312
  1.0 0.0 copy-start.1
  1.0 1.0 %copy-done.1 = bf16[1,2,2,256,256]{4,3,2,1,0:T(8,128)(2,1)S(1)} copy-done((bf16[1,2,2,256,256]{4,3,2,1,0:T(8,128)(2,1)S(1)}, bf16[1,2,2,256,256]{4,3,2,1,0:T(8,128)(2,1)}, u32[]{:S(2)}) %copy-start.1) | copy-done | bytes 524312
  2.1 0.0 copy-start.2
  2.1 0.9 %copy-done.2 = bf16[2,256,256]{2,1,0:T(8,128)(2,1)S(1)} copy-done((bf16[2,256,256]{2,1,0:T(8,128)(2,1)S(1)}, bf16[2,256,256]{2,1,0:T(8,128)(2,1)}, u32[]{:S(2)}) %copy-start.2) | copy-done | bytes 262168
  3.0 0.0 copy-start.3
  3.0 0.7 %copy-done.3 = f32[2,8,8]{2,1,0:T(8,128)S(1)} copy-done((f32[2,8,8]{2,1,0:T(8,128)S(1)}, f32[2,8,8]{2,1,0:T(8,128)}, u32[]{:S(2)}) %copy-start.3) | copy-done | bytes 536
  3.7 0.0 copy-start.4
  3.7 0.7 %copy-done.4 = f32[2,4,4]{2,1,0:T(4,128)S(1)} copy-done((f32[2,4,4]{2,1,0:T(4,128)S(1)}, f32[2,4,4]{2,1,0:T(4,128)}, u32[]{:S(2)}) %copy-start.4) | copy-done | bytes 152
  4.4 0.0 copy-start.5
  4.4 0.7 %copy-done.5 = f32[2,2,2]{2,1,0:T(2,128)S(1)} copy-done((f32[2,2,2]{2,1,0:T(2,128)S(1)}, f32[2,2,2]{2,1,0:T(2,128)}, u32[]{:S(2)}) %copy-start.5) | copy-done | bytes 56
  5.1 19.9 %shard_map.64 = f32[2,1,1,8,16,256]{5,4,3,2,1,0:T(8,128)S(1)} custom-call(bf16[1,2,1,1,512,256]{5,4,3,2,1,0:T(8,128)(2,1)S(1)} %copy-done, bf16[1,2,2,256,256]{4,3,2,1,0:T(8,128)(2,1)S(1)} %copy-done.1, bf16[2,256,256]{2,1,0:T(8,128)(2,1)S(1)} %copy-done.2, f32[2,4,4]{2,1,0:T(4,128)S(1)} %copy-done.4, f32[2,2,2]{2,1,0:T(2,128)S(1)} %copy-done.5, ...), custom_call_target="tpu_custom_call" | custom-call | tf_op jit(solution)/shard_map/pallas_call | solution.py:249
  25.1 0.7 %copy.8 = f32[2,1,1,8,16,256]{5,4,3,2,1,0:T(8,128)} copy(f32[2,1,1,8,16,256]{5,4,3,2,1,0:T(8,128)S(1)} %shard_map.64) | data formatting | bytes 524288
Async XLA Ops:
  0.0 1.0 %copy-start = (bf16[1,2,1,1,512,256]{5,4,3,2,1,0:T(8,128)(2,1)S(1)}, bf16[1,2,1,1,512,256]{5,4,3,2,1,0:T(8,128)(2,1)}, u32[]{:S(2)}) copy-start(bf16[1,2,1,1,512,256]{5,4,3,2,1,0:T(8,128)(2,1)} %x_hbm.1) | copy-start | bytes 1572868
  1.0 1.0 %copy-start.1 = (bf16[1,2,2,256,256]{4,3,2,1,0:T(8,128)(2,1)S(1)}, bf16[1,2,2,256,256]{4,3,2,1,0:T(8,128)(2,1)}, u32[]{:S(2)}) copy-start(bf16[1,2,2,256,256]{4,3,2,1,0:T(8,128)(2,1)} %gates_hbm.1) | copy-start | bytes 1572868
  2.1 0.9 %copy-start.2 = (bf16[2,256,256]{2,1,0:T(8,128)(2,1)S(1)}, bf16[2,256,256]{2,1,0:T(8,128)(2,1)}, u32[]{:S(2)}) copy-start(bf16[2,256,256]{2,1,0:T(8,128)(2,1)} %last_hbm.1) | copy-start | bytes 786436
  3.0 0.7 %copy-start.3 = (f32[2,8,8]{2,1,0:T(8,128)S(1)}, f32[2,8,8]{2,1,0:T(8,128)}, u32[]{:S(2)}) copy-start(f32[2,8,8]{2,1,0:T(8,128)} %mj_hbm.1) | copy-start | bytes 1540
  3.7 0.7 %copy-start.4 = (f32[2,4,4]{2,1,0:T(4,128)S(1)}, f32[2,4,4]{2,1,0:T(4,128)}, u32[]{:S(2)}) copy-start(f32[2,4,4]{2,1,0:T(4,128)} %m1_hbm.1) | copy-start | bytes 388
  4.4 0.7 %copy-start.5 = (f32[2,2,2]{2,1,0:T(2,128)S(1)}, f32[2,2,2]{2,1,0:T(2,128)}, u32[]{:S(2)}) copy-start(f32[2,2,2]{2,1,0:T(2,128)} %m2_hbm.1) | copy-start | bytes 100

commit v3 on v2

--- a/solution.py
+++ b/solution.py
@@ -270,7 +270,7 @@
             dma((2,)), dma((2,)), dma((2, na - 1)), dma((2, na - 1)),
         ],
         compiler_params=pltpu.CompilerParams(
-            collective_id=0, has_side_effects=True, vmem_limit_bytes=32 * 2**20
+            collective_id=0, has_side_effects=True, vmem_limit_bytes=56 * 2**20
         ),
     )(slice_tensors, slice_gates, last_gate, mix_first, mix_second, mix_joint)
 

time: 26.1 us -> 22.6 us (0.87)
  local copies, waits for them, and re-layouts: 5.8 us -> 1.67 us
  Pallas kernels: 19.9 us -> 20.8 us
    unnamed x13 -> x1, local copies, waits for them, and re-layouts: 5.8 us -> 1.67 us
    pallas_call x1, Pallas kernels: 19.9 us -> 20.8 us  [by_kernel(): pl.pallas_call(kernel, out_shape=jax.ShapeDtypeStruct((2, 1, 1, na * nb,...]
where the time goes in v3:
time: 22.6 us; the launch traced here: 22.5 us
  Pallas kernels  20.8 us (92%)
  local copies, waits for them, and re-layouts  1.67 us (7%)
    pallas_call x1, Pallas kernels, by_kernel(): pl.pallas_call(kernel, out_shape=jax.ShapeDtypeStruct((2, 1, 1, na * nb,...  20.8 us
    unnamed x1, local copies, waits for them, and re-layouts  1.67 us

profile of v3, /device:TPU:0, one launch (start us, length us, event | category | flops | bytes accessed | tf_op | source)
XLA Modules:
  0.0 22.5 jit_solution(14136326911158524147)
XLA Ops:
  0.0 20.8 %shard_map.64 = f32[2,1,1,8,16,256]{5,4,3,2,1,0:T(8,128)} custom-call(bf16[1,2,1,1,512,256]{5,4,3,2,1,0:T(8,128)(2,1)} %x_hbm.1, bf16[1,2,2,256,256]{4,3,2,1,0:T(8,128)(2,1)} %gates_hbm.1, bf16[2,256,256]{2,1,0:T(8,128)(2,1)} %last_hbm.1, f32[2,4,4]{2,1,0:T(4,128)} %m1_hbm.1, f32[2,2,2]{2,1,0:T(2,128)} %m2_hbm.1, f32[2,8,8]{2,1,0:T(8,128)} %mj_hbm.1), custom_call_target="tpu_custom_call" | custom-call | tf_op jit(solution)/shard_map/pallas_call | solution.py:249
  20.8 1.7 %copy.8 = f32[2,1,1,8,16,256]{5,4,3,2,1,0:T(8,128)} copy(f32[2,1,1,8,16,256]{5,4,3,2,1,0:T(8,128)} %shard_map.64) | data formatting | bytes 524288

commit v4 on v3

--- a/solution.py
+++ b/solution.py
@@ -111,19 +111,17 @@
     for copy in load_x:
         copy.wait()
 
-    chunks = ((0, 2), (1, 3))
     halves = (1 - bitb, bitb)
-    part = 2 * fine
+    part = fine
 
     def product(target):
         parts = []
         for z in range(2):
             pieces = []
             for half in halves:
-                for chunk in chunks:
-                    for u in chunk:
-                        start = u * (rows // na) + half * (rows // na // nb) + target * fine
-                        pieces.append(x_ref[z, pl.ds(pl.multiple_of(start, 16), fine), :])
+                for u in range(na):
+                    start = u * (rows // na) + half * (rows // na // nb) + target * fine
+                    pieces.append(x_ref[z, pl.ds(pl.multiple_of(start, 16), fine), :])
             parts.append(jnp.concatenate(pieces, axis=0))
         return dot(parts[0], gate[0]) + dot(parts[1], gate[1])
 
@@ -133,7 +131,7 @@
             device_id=device, device_id_type=MESH,
         )
 
-    a_copies, b_copies, c_copies, d_copies = [], [], [], []
+    a_copies, b_copies, c_copies, d_copies = [], {}, [], []
     for i, target in enumerate(((1 - y) * 2 + (1 - core), y * 2 + (1 - core))):
         send_a[i] = product(target).astype(BF16)
         if i == 0:
@@ -144,12 +142,13 @@
 
     total = product(at_y)
     a_copies[0].wait_recv()
-    for q in range(4):
+    order = (0, 1, 2, 4, 3, 5, 6, 7)
+    for q in order:
         rows_q = slice(q * part, (q + 1) * part)
         send_b[q] = (total[rows_q] + recv_a[0, rows_q].astype(F32)).astype(BF16)
         copy = remote(send_b.at[q], recv_b.at[q], b_send_sem.at[q], b_recv_sem.at[q], to_y)
         copy.start()
-        b_copies.append(copy)
+        b_copies[q] = copy
     total = product(cut)
     a_copies[1].wait_recv()
     total = total + recv_a[1].astype(F32)
@@ -165,8 +164,8 @@
     by_fine = fine.bit_length() - 1
     w_id = lax.broadcasted_iota(jnp.int32, (na * nb, lanes), 0)
     lane = lax.broadcasted_iota(jnp.int32, (na * nb, lanes), 1)
-    u_id = (((lane >> by_fine) & 1) << 1) | (lane >> (by_fine + 3))
-    d_id = (lane >> (by_fine + 1)) & 3
+    u_id = lane >> (by_fine + 2)
+    d_id = (lane >> by_fine) & 3
     mixed = [jnp.zeros((na * nb, lanes), F32), jnp.zeros((na * nb, lanes), F32)]
     for b in range(nb):
         first, joint = [], []
@@ -183,7 +182,7 @@
         mixed[0] += first[0] * joint[0] - first[1] * joint[1]
         mixed[1] += first[0] * joint[1] + first[1] * joint[0]
 
-    for h in range(2):
+    for h in range(na):
         send_c[h] = summed(h).astype(BF16)
         copy = remote(send_c.at[h], recv_c.at[h], c_send_sem.at[h], c_recv_sem.at[h], to_x)
         copy.start()
@@ -197,8 +196,8 @@
     ], axis=0).astype(BF16)
     last = wide(last_ref[0], last_ref[1])
 
-    for h in range(2):
-        own = summed(2 + h)
+    for h in range(na):
+        own = summed(na + h)
         own_r, own_i = own[:, :width], own[:, width:]
         c_copies[h].wait_recv()
         other = recv_c[h].astype(F32)
@@ -219,15 +218,16 @@
             copy.start()
             d_copies.append(copy)
 
-    columns = na * part
+    columns = 2 * na * part
     sums = None
-    for h in range(2):
-        for copy in d_copies[h * (na - 1):(h + 1) * (na - 1)]:
-            copy.wait_recv()
-        value = jnp.concatenate(
-            [send_d[h, bita // 2]] + [recv_d[h, s] for s in range(na - 1)], axis=0
-        )
-        more = dot(spread[:, h * columns:(h + 1) * columns], value)
+    for g in range(2):
+        pieces = []
+        for h in (2 * g, 2 * g + 1):
+            for copy in d_copies[h * (na - 1):(h + 1) * (na - 1)]:
+                copy.wait_recv()
+            pieces += [send_d[h, bita // 2]] + [recv_d[h, s] for s in range(na - 1)]
+        value = jnp.concatenate(pieces, axis=0)
+        more = dot(spread[:, g * columns:(g + 1) * columns], value)
         sums = more if sums is None else sums + more
     count = na * nb * fine
     real = (sums[:count, :width] - sums[count:, width:]).astype(BF16)
@@ -235,7 +235,7 @@
     result = dot(real, last[0]) + dot(imag, last[1])
     for z in range(2):
         out_ref[z, 0, 0] = result[:, z * width:(z + 1) * width].reshape(na * nb, fine, width)
-    for copy in a_copies + b_copies + c_copies + d_copies:
+    for copy in a_copies + [b_copies[q] for q in order] + c_copies + d_copies:
         copy.wait_send()
 
 
@@ -243,12 +243,12 @@
     rows, width = slice_tensors.shape[4:]
     na, nb, cuts = lax.axis_size("bita"), lax.axis_size("bitb"), lax.axis_size("cuts")
     fine = rows // (na * nb * cuts)
-    part = 2 * fine
+    part = fine
     hbm = pl.BlockSpec(memory_space=pltpu.MemorySpace.HBM)
     dma = pltpu.SemaphoreType.DMA
     return pl.pallas_call(
         kernel,
-        out_shape=jax.ShapeDtypeStruct((2, 1, 1, na * nb, fine, width), F32),
+        out_shape=pltpu.VMEM((2, 1, 1, na * nb, fine, width), F32),
         in_specs=[hbm] * 6,
         out_specs=pl.BlockSpec(memory_space=pltpu.VMEM),
         scratch_shapes=[
@@ -258,16 +258,16 @@
             pltpu.SMEM(mix_first.shape, F32),
             pltpu.SMEM(mix_second.shape, F32),
             pltpu.SMEM(mix_joint.shape, F32),
-            pltpu.VMEM((2, 4 * part, 2 * width), BF16),
-            pltpu.VMEM((2, 4 * part, 2 * width), BF16),
-            pltpu.VMEM((4, part, 2 * width), BF16),
-            pltpu.VMEM((4, part, 2 * width), BF16),
-            pltpu.VMEM((2, part, 2 * width), BF16),
-            pltpu.VMEM((2, part, 2 * width), BF16),
-            pltpu.VMEM((2, nb, part, 2 * width), BF16),
-            pltpu.VMEM((2, na - 1, part, 2 * width), BF16),
-            dma((8,)), dma((2,)), dma((2,)), dma((4,)), dma((4,)),
-            dma((2,)), dma((2,)), dma((2, na - 1)), dma((2, na - 1)),
+            pltpu.VMEM((2, 8 * part, 2 * width), BF16),
+            pltpu.VMEM((2, 8 * part, 2 * width), BF16),
+            pltpu.VMEM((8, part, 2 * width), BF16),
+            pltpu.VMEM((8, part, 2 * width), BF16),
+            pltpu.VMEM((na, part, 2 * width), BF16),
+            pltpu.VMEM((na, part, 2 * width), BF16),
+            pltpu.VMEM((na, nb, part, 2 * width), BF16),
+            pltpu.VMEM((na, na - 1, part, 2 * width), BF16),
+            dma((8,)), dma((2,)), dma((2,)), dma((8,)), dma((8,)),
+            dma((na,)), dma((na,)), dma((na, na - 1)), dma((na, na - 1)),
         ],
         compiler_params=pltpu.CompilerParams(
             collective_id=0, has_side_effects=True, vmem_limit_bytes=56 * 2**20

time: 22.6 us -> 20.8 us (0.920)
  local copies, waits for them, and re-layouts: 1.67 us -> 0.71 us
  Pallas kernels: 20.8 us -> 19.9 us
    unnamed x1, local copies, waits for them, and re-layouts: 1.67 us -> 0.71 us
    pallas_call x1, Pallas kernels: 20.8 us -> 19.9 us  [by_kernel(): pl.pallas_call(kernel, out_shape=pltpu.VMEM((2, 1, 1, na * nb, fine, widt...]
where the time goes in v4:
time: 20.8 us; the launch traced here: 20.6 us
  Pallas kernels  19.9 us (96%)
  local copies, waits for them, and re-layouts  0.71 us (3%)
    pallas_call x1, Pallas kernels, by_kernel(): pl.pallas_call(kernel, out_shape=pltpu.VMEM((2, 1, 1, na * nb, fine, widt...  19.9 us
    unnamed x1, local copies, waits for them, and re-layouts  0.71 us

profile of v4, /device:TPU:0, one launch (start us, length us, event | category | flops | bytes accessed | tf_op | source)
XLA Modules:
  0.0 20.6 jit_solution(9941001088824089368)
XLA Ops:
  0.0 19.9 %shard_map.64 = f32[2,1,1,8,16,256]{5,4,3,2,1,0:T(8,128)S(1)} custom-call(bf16[1,2,1,1,512,256]{5,4,3,2,1,0:T(8,128)(2,1)} %x_hbm.1, bf16[1,2,2,256,256]{4,3,2,1,0:T(8,128)(2,1)} %gates_hbm.1, bf16[2,256,256]{2,1,0:T(8,128)(2,1)} %last_hbm.1, f32[2,4,4]{2,1,0:T(4,128)} %m1_hbm.1, f32[2,2,2]{2,1,0:T(2,128)} %m2_hbm.1, f32[2,8,8]{2,1,0:T(8,128)} %mj_hbm.1), custom_call_target="tpu_custom_call" | custom-call | tf_op jit(solution)/shard_map/pallas_call | solution.py:249
  19.9 0.7 %copy.8 = f32[2,1,1,8,16,256]{5,4,3,2,1,0:T(8,128)} copy(f32[2,1,1,8,16,256]{5,4,3,2,1,0:T(8,128)S(1)} %shard_map.64) | data formatting | bytes 524288

commit v5 on v4

--- a/solution.py
+++ b/solution.py
@@ -82,7 +82,8 @@
     to_core = (at_core, bita, bitb)
     to_y = (at_y, bita, bitb)
     to_x = (cut, bita, 1 - bitb)
-    to_z = [(cut, lax.rem(bita + d, na), bitb) for d in range(1, na)]
+    at_z = [bita, bita + 1 - 2 * lax.rem(bita, 2), lax.rem(bita + 2, na), na - 1 - bita]
+    to_z = [(cut, at, bitb) for at in at_z[1:]]
 
     def load(src, dst, i):
         copy = pltpu.make_async_copy(src, dst, load_sem.at[i])
@@ -131,26 +132,34 @@
             device_id=device, device_id_type=MESH,
         )
 
-    a_copies, b_copies, c_copies, d_copies = [], {}, [], []
+    a_copies, b_copies, c_copies, d_copies = [], {}, [], {}
     for i, target in enumerate(((1 - y) * 2 + (1 - core), y * 2 + (1 - core))):
         send_a[i] = product(target).astype(BF16)
         if i == 0:
             pl.semaphore_wait(barrier, 6)
-        copy = remote(send_a.at[i], recv_a.at[i], a_send_sem.at[i], a_recv_sem.at[i], to_core)
-        copy.start()
-        a_copies.append(copy)
+        for half in range(2):
+            rows_half = pl.ds(half * na * part, na * part)
+            copy = remote(
+                send_a.at[i, rows_half], recv_a.at[i, rows_half],
+                a_send_sem.at[i, half], a_recv_sem.at[i, half], to_core,
+            )
+            copy.start()
+            a_copies.append(copy)
 
     total = product(at_y)
     a_copies[0].wait_recv()
-    order = (0, 1, 2, 4, 3, 5, 6, 7)
+    order = (0, 1, 2, 3, 4, 5, 6, 7)
     for q in order:
+        if q == na:
+            a_copies[1].wait_recv()
         rows_q = slice(q * part, (q + 1) * part)
         send_b[q] = (total[rows_q] + recv_a[0, rows_q].astype(F32)).astype(BF16)
         copy = remote(send_b.at[q], recv_b.at[q], b_send_sem.at[q], b_recv_sem.at[q], to_y)
         copy.start()
         b_copies[q] = copy
     total = product(cut)
-    a_copies[1].wait_recv()
+    a_copies[2].wait_recv()
+    a_copies[3].wait_recv()
     total = total + recv_a[1].astype(F32)
 
     def summed(q):
@@ -172,7 +181,7 @@
         for z in range(2):
             a_part = jnp.zeros((na * nb, lanes), F32)
             for d in range(na):
-                a_part = jnp.where(d_id == d, m1_ref[z, lax.rem(bita + d, na), b * 2 + low], a_part)
+                a_part = jnp.where(d_id == d, m1_ref[z, at_z[d], b * 2 + low], a_part)
             j_part = jnp.zeros((na * nb, lanes), F32)
             for u in range(na):
                 for w in range(na * nb):
@@ -195,6 +204,14 @@
         jnp.where(same, mixed[z][w:w + 1], 0.0) for z in range(2) for w in range(na * nb)
     ], axis=0).astype(BF16)
     last = wide(last_ref[0], last_ref[1])
+
+    def d_start(src, h, slot, d):
+        copy = remote(
+            src, recv_d.at[h, slot - 1], d_send_sem.at[h, slot - 1],
+            d_recv_sem.at[h, slot - 1], to_z[d - 1],
+        )
+        copy.start()
+        d_copies[h, slot] = copy
 
     for h in range(na):
         own = summed(na + h)
@@ -209,22 +226,20 @@
                 own_r * kr - own_i * ki + other_r * pr - other_i * pi,
                 own_r * ki + own_i * kr + other_r * pi + other_i * pr,
             ], axis=1).astype(BF16)
-        for d in (2, 1, 3):
-            to = lax.rem(bita + d, na)
-            copy = remote(
-                send_d.at[h, to // 2], recv_d.at[h, na - 1 - d], d_send_sem.at[h, d - 1],
-                d_recv_sem.at[h, na - 1 - d], (cut, to, bitb),
-            )
-            copy.start()
-            d_copies.append(copy)
+        for d in ((2, 1) if h < 2 else (3, 2, 1)):
+            d_start(send_d.at[h, at_z[d] // 2], h, d, d)
+        if h >= 2:
+            d_copies[h - 2, 2].wait_recv()
+            d_start(recv_d.at[h - 2, 1], h - 2, 3, 1)
 
     columns = 2 * na * part
     sums = None
     for g in range(2):
         pieces = []
         for h in (2 * g, 2 * g + 1):
-            for copy in d_copies[h * (na - 1):(h + 1) * (na - 1)]:
-                copy.wait_recv()
+            for slot in range(1, na):
+                if h >= 2 or slot != 2:
+                    d_copies[h, slot].wait_recv()
             pieces += [send_d[h, bita // 2]] + [recv_d[h, s] for s in range(na - 1)]
         value = jnp.concatenate(pieces, axis=0)
         more = dot(spread[:, g * columns:(g + 1) * columns], value)
@@ -235,7 +250,7 @@
     result = dot(real, last[0]) + dot(imag, last[1])
     for z in range(2):
         out_ref[z, 0, 0] = result[:, z * width:(z + 1) * width].reshape(na * nb, fine, width)
-    for copy in a_copies + [b_copies[q] for q in order] + c_copies + d_copies:
+    for copy in a_copies + list(b_copies.values()) + c_copies + list(d_copies.values()):
         copy.wait_send()
 
 
@@ -266,7 +281,7 @@
             pltpu.VMEM((na, part, 2 * width), BF16),
             pltpu.VMEM((na, nb, part, 2 * width), BF16),
             pltpu.VMEM((na, na - 1, part, 2 * width), BF16),
-            dma((8,)), dma((2,)), dma((2,)), dma((8,)), dma((8,)),
+            dma((8,)), dma((2, 2)), dma((2, 2)), dma((8,)), dma((8,)),
             dma((na,)), dma((na,)), dma((na, na - 1)), dma((na, na - 1)),
         ],
         compiler_params=pltpu.CompilerParams(

time: 20.8 us -> 21.3 us (1.024)
  Pallas kernels: 19.9 us -> 20.4 us
    pallas_call x1, Pallas kernels: 19.9 us -> 20.4 us  [by_kernel(): pl.pallas_call(kernel, out_shape=pltpu.VMEM((2, 1, 1, na * nb, fine, widt...]
where the time goes in v5:
time: 21.3 us; the launch traced here: 21.2 us
  Pallas kernels  20.4 us (96%)
  local copies, waits for them, and re-layouts  0.71 us (3%)
    pallas_call x1, Pallas kernels, by_kernel(): pl.pallas_call(kernel, out_shape=pltpu.VMEM((2, 1, 1, na * nb, fine, widt...  20.4 us
    unnamed x1, local copies, waits for them, and re-layouts  0.71 us

profile of v5, /device:TPU:0, one launch (start us, length us, event | category | flops | bytes accessed | tf_op | source)
XLA Modules:
  0.0 21.2 jit_solution(16713383697325900286)
XLA Ops:
  0.0 20.4 %shard_map.64 = f32[2,1,1,8,16,256]{5,4,3,2,1,0:T(8,128)S(1)} custom-call(bf16[1,2,1,1,512,256]{5,4,3,2,1,0:T(8,128)(2,1)} %x_hbm.1, bf16[1,2,2,256,256]{4,3,2,1,0:T(8,128)(2,1)} %gates_hbm.1, bf16[2,256,256]{2,1,0:T(8,128)(2,1)} %last_hbm.1, f32[2,4,4]{2,1,0:T(4,128)} %m1_hbm.1, f32[2,2,2]{2,1,0:T(2,128)} %m2_hbm.1, f32[2,8,8]{2,1,0:T(8,128)} %mj_hbm.1), custom_call_target="tpu_custom_call" | custom-call | tf_op jit(solution)/shard_map/pallas_call | solution.py:264
  20.4 0.7 %copy.8 = f32[2,1,1,8,16,256]{5,4,3,2,1,0:T(8,128)} copy(f32[2,1,1,8,16,256]{5,4,3,2,1,0:T(8,128)S(1)} %shard_map.64) | data formatting | bytes 524288

commit v6 on v5

--- a/solution.py
+++ b/solution.py
@@ -228,13 +228,13 @@
             ], axis=1).astype(BF16)
         for d in ((2, 1) if h < 2 else (3, 2, 1)):
             d_start(send_d.at[h, at_z[d] // 2], h, d, d)
-        if h >= 2:
-            d_copies[h - 2, 2].wait_recv()
-            d_start(recv_d.at[h - 2, 1], h - 2, 3, 1)
+    for h in range(2):
+        d_copies[h, 2].wait_recv()
+        d_start(recv_d.at[h, 1], h, 3, 1)
 
     columns = 2 * na * part
     sums = None
-    for g in range(2):
+    for g in (1, 0):
         pieces = []
         for h in (2 * g, 2 * g + 1):
             for slot in range(1, na):

time: 21.3 us -> 20.8 us (0.977)
  Pallas kernels: 20.4 us -> 20 us
    pallas_call x1, Pallas kernels: 20.4 us -> 20 us  [by_kernel(): pl.pallas_call(kernel, out_shape=pltpu.VMEM((2, 1, 1, na * nb, fine, widt...]
where the time goes in v6:
time: 20.8 us; the launch traced here: 20.7 us
  Pallas kernels  20 us (96%)
  local copies, waits for them, and re-layouts  0.71 us (3%)
    pallas_call x1, Pallas kernels, by_kernel(): pl.pallas_call(kernel, out_shape=pltpu.VMEM((2, 1, 1, na * nb, fine, widt...  20 us
    unnamed x1, local copies, waits for them, and re-layouts  0.71 us

profile of v6, /device:TPU:0, one launch (start us, length us, event | category | flops | bytes accessed | tf_op | source)
XLA Modules:
  0.0 20.7 jit_solution(8984941989897786157)
XLA Ops:
  0.0 20.0 %shard_map.64 = f32[2,1,1,8,16,256]{5,4,3,2,1,0:T(8,128)S(1)} custom-call(bf16[1,2,1,1,512,256]{5,4,3,2,1,0:T(8,128)(2,1)} %x_hbm.1, bf16[1,2,2,256,256]{4,3,2,1,0:T(8,128)(2,1)} %gates_hbm.1, bf16[2,256,256]{2,1,0:T(8,128)(2,1)} %last_hbm.1, f32[2,4,4]{2,1,0:T(4,128)} %m1_hbm.1, f32[2,2,2]{2,1,0:T(2,128)} %m2_hbm.1, f32[2,8,8]{2,1,0:T(8,128)} %mj_hbm.1), custom_call_target="tpu_custom_call" | custom-call | tf_op jit(solution)/shard_map/pallas_call | solution.py:264
  20.0 0.7 %copy.8 = f32[2,1,1,8,16,256]{5,4,3,2,1,0:T(8,128)} copy(f32[2,1,1,8,16,256]{5,4,3,2,1,0:T(8,128)S(1)} %shard_map.64) | data formatting | bytes 524288

commit v7 on v6

--- a/solution.py
+++ b/solution.py
@@ -165,6 +165,12 @@
     def summed(q):
         b_copies[q].wait_recv()
         return total[q * part:(q + 1) * part] + recv_b[q].astype(F32)
+
+    for h in range(na):
+        send_c[h] = summed(h).astype(BF16)
+        copy = remote(send_c.at[h], recv_c.at[h], c_send_sem.at[h], c_recv_sem.at[h], to_x)
+        copy.start()
+        c_copies.append(copy)
 
     for copy in load_rest:
         copy.wait()
@@ -190,12 +196,6 @@
             joint.append(j_part)
         mixed[0] += first[0] * joint[0] - first[1] * joint[1]
         mixed[1] += first[0] * joint[1] + first[1] * joint[0]
-
-    for h in range(na):
-        send_c[h] = summed(h).astype(BF16)
-        copy = remote(send_c.at[h], recv_c.at[h], c_send_sem.at[h], c_recv_sem.at[h], to_x)
-        copy.start()
-        c_copies.append(copy)
 
     same = (
         lax.broadcasted_iota(jnp.int32, (fine, lanes), 1) & (fine - 1)

time: 20.8 us -> 20.8 us (level)
  no operation moved by 1% of the time
where the time goes in v7:
time: 20.8 us; the launch traced here: 20.7 us
  Pallas kernels  20 us (96%)
  local copies, waits for them, and re-layouts  0.71 us (3%)
    pallas_call x1, Pallas kernels, by_kernel(): pl.pallas_call(kernel, out_shape=pltpu.VMEM((2, 1, 1, na * nb, fine, widt...  20 us
    unnamed x1, local copies, waits for them, and re-layouts  0.71 us

profile of v7, /device:TPU:0, one launch (start us, length us, event | category | flops | bytes accessed | tf_op | source)
XLA Modules:
  0.0 20.7 jit_solution(1404357547828876948)
XLA Ops:
  0.0 20.0 %shard_map.64 = f32[2,1,1,8,16,256]{5,4,3,2,1,0:T(8,128)S(1)} custom-call(bf16[1,2,1,1,512,256]{5,4,3,2,1,0:T(8,128)(2,1)} %x_hbm.1, bf16[1,2,2,256,256]{4,3,2,1,0:T(8,128)(2,1)} %gates_hbm.1, bf16[2,256,256]{2,1,0:T(8,128)(2,1)} %last_hbm.1, f32[2,4,4]{2,1,0:T(4,128)} %m1_hbm.1, f32[2,2,2]{2,1,0:T(2,128)} %m2_hbm.1, f32[2,8,8]{2,1,0:T(8,128)} %mj_hbm.1), custom_call_target="tpu_custom_call" | custom-call | tf_op jit(solution)/shard_map/pallas_call | solution.py:264
  20.0 0.7 %copy.8 = f32[2,1,1,8,16,256]{5,4,3,2,1,0:T(8,128)} copy(f32[2,1,1,8,16,256]{5,4,3,2,1,0:T(8,128)S(1)} %shard_map.64) | data formatting | bytes 524288
